TPU v7x, 1024 devices: a whole 4x8x16 slice. The times are simulated.
1024 devices in a mesh: dp: 4 (over y_hi), edata: 4 (over x), expert: 64 (over z, y_lo, core).
Axes of the slice: x: 4, y: 8 (y_hi: 4, y_lo: 2; y = y_hi * 2 + y_lo), z: 16, core: 2. Of those that a mesh axis runs over, the one named last changes fastest.
Arguments:
- out_grad: bfloat16 [131072, 3584], P(('dp', 'edata', 'expert')), may hold values from -4 to 4
- route_ids: int32 [131072, 8], P(('dp', 'edata', 'expert')), may hold values from 0 to 255, as said below
- router_logits: float32 [131072, 8], P(('dp', 'edata', 'expert')), may hold values from -8 to 8
- hidden: bfloat16 [16, 64, 192, 1024], P(('dp', 'edata'), 'expert'), may hold values from -6 to 6
- down_weight: bfloat16 [3584, 64, 1024], P(None, 'expert'), may hold values from -0.375 to 0.375
Outputs:
- grad_down: bfloat16 [3584, 64, 1024], P(('dp', 'edata'), 'expert')
- grad_hidden: bfloat16 [16, 64, 192, 1024], P(('dp', 'edata'), 'expert')
- logit_grad: float32 [131072, 8], P(('dp', 'edata', 'expert'))
Inputs may be any that keep to these rules, and one draw needn't show every extreme that they name: `route_ids`: each row names 8 different experts. Within the rows of one device no expert below 64 is named more than 3 times, and on every device one of them is named exactly 3 times.
All inputs are finite; a program needn't handle non-finite values.
Results may differ from a plain program's by a relative error of at most 0.019.
Values may be sent and summed in bfloat16 or wider, within the bound.
A program may use at most 64 MiB of HBM per device.

v0:
```python
import jax
import jax.numpy as jnp
from jax import lax
from jax.sharding import PartitionSpec as P


def on_device(out_grad, route_ids, router_logits, hidden, down_weight):
    tok_rows, top_count = route_ids.shape
    features = out_grad.shape[1]
    local_experts = down_weight.shape[1]
    owners = lax.axis_size("expert")
    slot_count = hidden.shape[2]
    capacity = slot_count // owners
    experts_all = local_experts * owners
    block_len = local_experts * capacity
    buffer_len = owners * block_len
    scores = jax.nn.sigmoid(router_logits)
    score_sum = jnp.sum(scores, axis=1, keepdims=True)
    combine = 2.5 * scores / score_sum
    combine_send = combine.astype(jnp.bfloat16)
    flat_ids = route_ids.reshape(-1)
    in_window = flat_ids < experts_all
    onehot = (flat_ids[:, None] == jnp.arange(experts_all, dtype=jnp.int32)[None, :]).astype(
        jnp.int32
    )
    rank_in_device = jnp.sum((jnp.cumsum(onehot, axis=0) - 1) * onehot, axis=1)
    position = (
        flat_ids // local_experts * block_len + flat_ids % local_experts * capacity + rank_in_device
    )
    position = jnp.where(in_window, position, buffer_len)
    select = position[None, :] == jnp.arange(buffer_len, dtype=jnp.int32)[:, None]
    select_bf = select.astype(jnp.bfloat16)
    token_select = jnp.any(select.reshape(buffer_len, tok_rows, top_count), axis=2).astype(
        jnp.bfloat16
    )
    send_rows = jnp.dot(token_select, out_grad, preferred_element_type=jnp.float32).astype(
        jnp.bfloat16
    )
    send_weight = jnp.dot(
        select_bf, combine_send.reshape(-1), preferred_element_type=jnp.float32
    ).astype(jnp.bfloat16)
    send_rows = send_rows.reshape(owners, block_len, features)
    send_weight = send_weight.reshape(owners, block_len)
    arrived_rows, arrived_weight = (
        lax.all_to_all(send_rows, "expert", split_axis=0, concat_axis=0, tiled=True),
        lax.all_to_all(send_weight, "expert", split_axis=0, concat_axis=0, tiled=True),
    )
    slot_rows = arrived_rows.reshape(owners, local_experts, capacity, features).transpose(
        1, 0, 2, 3
    )
    slot_rows = slot_rows.reshape(local_experts, slot_count, features)
    weight = arrived_weight.reshape(owners, local_experts, capacity).transpose(1, 0, 2)
    weight = weight.reshape(local_experts, slot_count).astype(jnp.float32)
    local_hidden = hidden[0]
    projected = jnp.einsum(
        "esd,dej->esj", slot_rows, down_weight, preferred_element_type=jnp.float32
    )
    grad_hidden = (weight[:, :, None] * projected).astype(jnp.bfloat16)[None]
    scaled = (weight[:, :, None] * slot_rows.astype(jnp.float32)).astype(jnp.bfloat16)
    slot_grad = jnp.sum(local_hidden.astype(jnp.float32) * projected, axis=2)
    return_block = (
        slot_grad.reshape(local_experts, owners, capacity)
        .transpose(1, 0, 2)
        .reshape(owners, block_len)
    )
    returned = lax.all_to_all(return_block, "expert", split_axis=0, concat_axis=0, tiled=True)
    safe_position = jnp.where(in_window, position, 0)
    picked = jnp.take(returned.reshape(-1), safe_position)
    combine_grad = jnp.where(in_window, picked, 0.0).reshape(tok_rows, top_count)
    weighted_mean = jnp.sum(combine_grad * scores, axis=1, keepdims=True) / score_sum
    logit_grad = scores * (1.0 - scores) * (2.5 / score_sum) * (combine_grad - weighted_mean)
    grad_down = lax.psum_scatter(
        jnp.einsum("esd,esj->dej", scaled, local_hidden, preferred_element_type=jnp.float32).astype(
            jnp.bfloat16
        ),
        ("dp", "edata"),
        scatter_dimension=0,
        tiled=True,
    )
    return (grad_down, grad_hidden, logit_grad)


def solution(mesh):
    in_specs = (
        P(("dp", "edata", "expert"), None),
        P(("dp", "edata", "expert"), None),
        P(("dp", "edata", "expert"), None),
        P(("dp", "edata"), "expert", None, None),
        P(None, "expert", None),
    )
    out_specs = (
        P(("dp", "edata"), "expert", None),
        P(("dp", "edata"), "expert", None, None),
        P(("dp", "edata", "expert"), None),
    )
    return jax.shard_map(
        on_device, mesh=mesh, in_specs=in_specs, out_specs=out_specs, check_vma=False
    )
```

profile of v0, /device:TPU:1, one launch (start us, length us, event | category | flops | bytes accessed | tf_op | source)
XLA Modules:
  0.0 346.8 jit_solution(9734232846288842991)
XLA Ops:
  7.2 0.9 copy.38
  8.1 0.1 reshape.228
  8.2 0.1 eq.48
  8.3 18.0 %reduce-window.6 = s32[64,8,128]{2,1,0:T(8,128)S(1)} reduce-window(s32[64,8,128]{2,1,0:T(8,128)S(1)} %fusion.13, s32[]{:T(128)} %constant.59.clone.1), window={size=1x1x128 pad=0_0x0_0x127_0}, to_apply=%region_0.0 | reduce-window | flops 8323072 | bytes 524292 | tf_op jit(solution)/shard_map/reduce-window
  26.3 0.1 slice.10
  26.4 0.1 copy.40
  26.6 0.1 copy.41
  26.7 0.1 add_add_fusion
  26.8 0.1 fusion.12
  26.9 0.1 reduce_sum.42
  27.0 0.6 add_select_fusion
  27.7 0.3 fusion.6
  27.9 0.5 convolution_convert_fusion.1
  28.5 2.2 reshape.231
  30.6 22.0 %all-to-all-start.1 = ((bf16[64,3,3584]{2,1,0:T(4,128)(2,1)}), bf16[64,3,3584]{2,1,0:T(4,128)(2,1)S(1)}, u32[]{:S(2)}, u32[]{:S(2)}) async-start(bf16[64,3,3584]{2,1,0:T(4,128)(2,1)} %reshape.231), calls=%async_computation.1 | async-start | bytes 3670016 | tf_op jit(solution)/shard_map/all_to_all | solution.py:45
  52.6 0.1 copy.46
  52.7 0.1 lt.56
  52.8 0.1 copy.47
  52.9 0.1 add.88
  53.0 0.6 add_select_fusion.1
  53.6 0.6 compare_select_fusion
  54.2 85.8 %all-to-all-done.1 = bf16[64,3,3584]{2,1,0:T(4,128)(2,1)S(1)} async-done(((bf16[64,3,3584]{2,1,0:T(4,128)(2,1)}), bf16[64,3,3584]{2,1,0:T(4,128)(2,1)S(1)}, u32[]{:S(2)}, u32[]{:S(2)}) %all-to-all-start.1) | async-done | bytes 1376288 | tf_op jit(solution)/shard_map/all_to_all | solution.py:45
  140.0 2.3 reshape.233
  142.4 5.7 %multiply_reduce_fusion = (f32[192]{0:T(256)}, f32[192,1024]{1,0:T(8,128)S(1)}) fusion(bf16[1,1,192,1024]{3,2,1,0:T(8,128)(2,1)} %param.8, bf16[192,3584]{1,0:T(8,128)(2,1)} %reshape.233, bf16[3584,1,1024]{2,0,1:T(8,128)(2,1)} %param.9), kind=kOutput, calls=%fused_computation.9 | convolution fusion | flops 1409875712 | bytes 9896704 | tf_op jit(solution)/shard_map/esd,dej->esj/dot_general | solution.py:55
  148.1 1.4 all_to_all.18
  149.6 7.7 %all-to-all-start.2 = ((f32[64,1,3]{2,1,0:T(1,128)}), f32[64,1,3]{2,1,0:T(1,128)}, u32[]{:S(2)}, u32[]{:S(2)}) async-start(f32[64,1,3]{2,1,0:T(1,128)} %bitcast.43), calls=%async_computation.3 | async-start | bytes 65536 | tf_op jit(solution)/shard_map/all_to_all | solution.py:66
  157.3 0.6 broadcast_clamp_fusion
  157.9 12.6 %all-to-all-done.2 = f32[64,1,3]{2,1,0:T(1,128)} async-done(((f32[64,1,3]{2,1,0:T(1,128)}), f32[64,1,3]{2,1,0:T(1,128)}, u32[]{:S(2)}, u32[]{:S(2)}) %all-to-all-start.2) | async-done | bytes 800 | tf_op jit(solution)/shard_map/all_to_all | solution.py:66
  170.4 0.5 broadcast.302
  171.0 2.1 reduce.9
  173.1 0.9 reshape.235
  174.0 11.4 %gather_fusion = f32[1024]{0:T(1024)} fusion(f32[192]{0:T(256)S(1)} %reshape.235, s32[1024]{0:T(1024)} %broadcast_clamp_fusion), kind=kCustom, calls=%fused_computation | custom fusion | bytes 12288 | tf_op jit(solution)/shard_map/jit(_take)/gather | solution.py:68
  185.4 1.4 gather.7
  186.8 0.9 copy.48
  187.7 0.6 fusion.15
  188.3 1.4 copy.42
  189.7 0.9 reshape.246
  190.6 0.9 fusion.7
  191.5 0.8 all_to_all.20
  192.3 5.3 %all-to-all-start = ((bf16[64,1,3]{2,1,0:T(2,128)(2,1)}), bf16[64,1,3]{2,1,0:T(2,128)(2,1)}, u32[]{:S(2)}, u32[]{:S(2)}) async-start(bf16[64,1,3]{2,1,0:T(2,128)(2,1)} %all_to_all.20), calls=%async_computation | async-start | bytes 65536 | tf_op jit(solution)/shard_map/all_to_all | solution.py:46
  197.6 0.0 reduce-scatter.2.cloned.1.call-start
  197.7 2.6 reshape.237
  200.2 10.6 %all-to-all-done = bf16[64,1,3]{2,1,0:T(2,128)(2,1)} async-done(((bf16[64,1,3]{2,1,0:T(2,128)(2,1)}), bf16[64,1,3]{2,1,0:T(2,128)(2,1)}, u32[]{:S(2)}, u32[]{:S(2)}) %all-to-all-start) | async-done | bytes 416 | tf_op jit(solution)/shard_map/all_to_all | solution.py:46
  210.8 0.9 convert_reduce_fusion
  211.7 0.1 reshape.236
  211.8 7.0 %fusion.2 = bf16[3584,1,1024]{2,0,1:T(8,128)(2,1)} fusion(f32[1,192,1,1,1,1,3584]{6,1,5,4,3,2,0:T(8,128)} %reshape.237, f32[192]{0:T(256)S(1)} %reshape.236, bf16[1,1,192,1024]{3,2,1,0:T(8,128)(2,1)} %param.8), kind=kOutput, calls=%fused_computation.4 | convolution fusion | flops 1414332416 | bytes 10486528 | tf_op jit(solution)/shard_map/esd,esj->dej/dot_general | solution.py:73
  218.8 0.9 fusion.8
  219.7 120.2 %reduce-scatter.2.cloned.1.call-done = bf16[224,1,1024]{2,0,1:T(8,128)(2,1)} async-done(((bf16[3584,1,1024]{2,0,1:T(8,128)(2,1)}), bf16[224,1,1024]{2,0,1:T(8,128)(2,1)}) %reduce-scatter.2.cloned.1.call-update) | async-done | bytes 458768 | tf_op jit(solution)/shard_map/reduce_scatter | solution.py:72
  (20 shorter events, 0.2 us)
Async XLA Ops:
  7.2 20.8 %copy-start = (bf16[128,3584]{1,0:T(8,128)(2,1)S(1)}, bf16[128,3584]{1,0:T(8,128)(2,1)}, u32[]{:S(2)}) copy-start(bf16[128,3584]{1,0:T(8,128)(2,1)} %param.5) | copy-start | bytes 2752516
  7.2 19.9 %copy-start.1 = (s32[128,8]{0,1:T(8,128)S(1)}, s32[128,8]{0,1:T(8,128)}, u32[]{:S(2)}) copy-start(s32[128,8]{0,1:T(8,128)} %param.6) | copy-start | bytes 12292
  30.6 22.0 %copy-start.3 = (pred[128,8]{0,1:T(8,128)(4,1)S(1)}, pred[128,8]{0,1:T(8,128)(4,1)}, u32[]{:S(2)}) copy-start(pred[128,8]{0,1:T(8,128)(4,1)} %get-tuple-element.15) | copy-start | bytes 3076
  30.6 109.4 %all-to-all-start.1 = ((bf16[64,3,3584]{2,1,0:T(4,128)(2,1)}), bf16[64,3,3584]{2,1,0:T(4,128)(2,1)S(1)}, u32[]{:S(2)}, u32[]{:S(2)}) async-start(bf16[64,3,3584]{2,1,0:T(4,128)(2,1)} %reshape.231), calls=%async_computation.1 | async-start | bytes 3670016 | tf_op jit(solution)/shard_map/all_to_all | solution.py:45
  142.4 14.9 %copy-start.5 = (s32[1024,1]{0,1:T(1,128)S(1)}, s32[1024,1]{0,1:T(1,128)}, u32[]{:S(2)}) copy-start(s32[1024,1]{0,1:T(1,128)} %compare_select_fusion) | copy-start | bytes 12292
  148.1 39.5 %copy-start.2 = (f32[128,8]{0,1:T(8,128)S(1)}, f32[128,8]{0,1:T(8,128)}, u32[]{:S(2)}) copy-start(f32[128,8]{0,1:T(8,128)} %param.7) | copy-start | bytes 12292
  148.1 39.5 %copy-start.4 = (pred[128,8]{0,1:T(8,128)(4,1)S(1)}, pred[128,8]{0,1:T(8,128)(4,1)}, u32[]{:S(2)}) copy-start(pred[128,8]{0,1:T(8,128)(4,1)} %get-tuple-element.15) | copy-start | bytes 3076
  149.6 20.9 %all-to-all-start.2 = ((f32[64,1,3]{2,1,0:T(1,128)}), f32[64,1,3]{2,1,0:T(1,128)}, u32[]{:S(2)}, u32[]{:S(2)}) async-start(f32[64,1,3]{2,1,0:T(1,128)} %bitcast.43), calls=%async_computation.3 | async-start | bytes 65536 | tf_op jit(solution)/shard_map/all_to_all | solution.py:66
  192.3 18.5 %all-to-all-start = ((bf16[64,1,3]{2,1,0:T(2,128)(2,1)}), bf16[64,1,3]{2,1,0:T(2,128)(2,1)}, u32[]{:S(2)}, u32[]{:S(2)}) async-start(bf16[64,1,3]{2,1,0:T(2,128)(2,1)} %all_to_all.20), calls=%async_computation | async-start | bytes 65536 | tf_op jit(solution)/shard_map/all_to_all | solution.py:46
  197.6 142.3 %reduce-scatter.2.cloned.1.call-start = ((), (), s32[]{:S(2)}) async-start(), calls=%async_computation.4 | async-start | bytes 7798784 | tf_op jit(solution)/shard_map/reduce_scatter | solution.py:72
Sparse Core Ops, SparseCore 0:
  219.0 120.9 reduce-scatter.1
where the time goes:
time: 348 us; the launch traced here: 347 us
  waiting for transfers between devices  229 us (66%)
  starting transfers between devices  35 us (10%)
  local copies, waits for them, and re-layouts  28.8 us (8%)
  other arithmetic  25.4 us (7%)
  matrix products  14.2 us (4%)
  between operations  14.2 us (4%)
    reduce_scatter x1, waiting for transfers between devices, on_device(): lax.psum_scatter(jnp.einsum('esd,esj->dej', scaled, local_hidden, preferr...  120 us
    all_to_all x1, waiting for transfers between devices, on_device(): lax.all_to_all(send_rows, 'expert', split_axis=0, concat_axis=0, tiled=True)  85.8 us
    all_to_all x1, starting transfers between devices, on_device(): lax.all_to_all(send_rows, 'expert', split_axis=0, concat_axis=0, tiled=True)  22 us
    another operation x2, other arithmetic  18 us
    gather x3, local copies, waits for them, and re-layouts, on_device(): picked = jnp.take(returned.reshape(-1), safe_position)  13.7 us
    all_to_all x1, waiting for transfers between devices, on_device(): lax.all_to_all(return_block, 'expert', split_axis=0, concat_axis=0, tiled...  12.6 us
    all_to_all x1, waiting for transfers between devices, on_device(): lax.all_to_all(send_weight, 'expert', split_axis=0, concat_axis=0, tiled=...  10.6 us
    all_to_all x1, starting transfers between devices, on_device(): lax.all_to_all(return_block, 'expert', split_axis=0, concat_axis=0, tiled...  7.68 us
  transfers between devices with their start and end apart: 4, of which 4 were waited for; matrix products, arithmetic and copies ran while one was open for 2% of the time, Pallas kernels for 0%

commit v1 on v0

v1 whole, which is shorter than its diff:
```python
import jax
import jax.numpy as jnp
from jax import lax
from jax.experimental import pallas as pl
from jax.experimental.pallas import tpu as pltpu
from jax.sharding import PartitionSpec as P

MESH = pl.DeviceIdType.MESH
BF = jnp.bfloat16
F32 = jnp.float32
NZ = 16
NJ = 4
NX = 4
NY = 4
CAP = 3
TOK = 128
TOP = 8
D = 3584
H = 1024
SLOTS = NZ * NJ * CAP
PLANE_ROWS = NZ * CAP
ZROWS = 16
CH = 512
NCH = D // CH
FOLD = CH // 128 - 1
BLK = D // NY
OWN = BLK // NX
PAD = 256
LAG = 3
OFFS = [8, 7, 9, 6, 10, 5, 11, 4, 12, 3, 13, 2, 14, 1, 15]


def iota(shape, axis):
    return lax.broadcasted_iota(jnp.int32, shape, axis)


def dot(a, b):
    return jnp.dot(a, b, preferred_element_type=F32)


def exact_dot(a, b):
    return jnp.dot(a, b, preferred_element_type=F32, precision=lax.Precision.HIGHEST)


def slot_parts(row):
    j = (row * 1366) >> 16
    rest = row - 48 * j
    z = (rest * 43) >> 7
    return j, z, rest - 3 * z


def fold_slot(row, part):
    z = row >> 4
    q = row & 15
    if part == 0:
        valid, s = q < 12, q
    else:
        valid, s = q >= 12, 4 * (part - 1) + (q - 12)
    j = (s * 11) >> 5
    return jnp.where(valid, z * NJ + j, -1), s - 3 * j


def named(ids, weights, expert):
    rows = expert.shape[0]
    count = jnp.zeros((rows, TOK), F32)
    weight = jnp.zeros((rows, TOK), F32)
    for k in range(TOP):
        hit = ids[k : k + 1, :] == expert
        count = count + jnp.where(hit, 1.0, 0.0)
        weight = weight + jnp.where(hit, weights[k : k + 1, :], 0.0)
    before = (iota((TOK, TOK), 0) < iota((TOK, TOK), 1)).astype(F32).astype(BF)
    rank = dot(count.astype(BF), before)
    return count, weight, rank


def kernel(
    og_hbm, ids_hbm, logit_hbm, hid_hbm, w_hbm,
    gd_hbm, gh_hbm, lg_hbm,
    og_s, ids_s, logit_s, hid_s, w_s, sel_s, unf_s, h4, zs, zr, ps, ar, xs, xr, ys, yr, proj,
    cnt_s, rank_s, r1s, r1r, r2s, r2r, gd_s, gh_s, lg_s,
    in_sem, out_sem, hs_sem, hr_sem, zs_sem, zr_sem, zl_sem, ps_sem, pr_sem, pl_sem,
    xs_sem, xr_sem, xl_sem, ys_sem, yr_sem, r_sem,
):
    dp = lax.axis_index("dp")
    ed = lax.axis_index("edata")
    ex = lax.axis_index("expert")
    z = ex // NJ
    j = ex % NJ
    core = ex % 2

    def at_z(h):
        return lax.rem(z + h, NZ)

    def at_j(h):
        return lax.rem(j + h, NJ)

    def at_x(h):
        return lax.rem(ed + h, NX)

    def to_z(zt):
        return {"expert": zt * NJ + j}

    def to_j(jt):
        return {"expert": z * NJ + jt}

    def owner(b, c):
        step = (2, 1, 3, 0)[b] if not isinstance(c, int) else ((2, 1, 3, 0), (2, 3, 1, 0))[c][b]
        if not isinstance(c, int) and b in (1, 2):
            step = jnp.where(c == 0, step, 4 - step)
        return lax.rem(dp + step, NY)

    def remote(src, dst, ssem, rsem, where):
        return pltpu.make_async_remote_copy(
            src_ref=src, dst_ref=dst, send_sem=ssem, recv_sem=rsem, device_id=where, device_id_type=MESH
        )

    barrier = pltpu.get_barrier_semaphore()
    for h in OFFS:
        pl.semaphore_signal(barrier, inc=1, device_id=to_z(at_z(h)), device_id_type=MESH)
    for h in range(1, 4):
        pl.semaphore_signal(barrier, inc=1, device_id=to_j(at_j(h)), device_id_type=MESH)
        pl.semaphore_signal(barrier, inc=1, device_id={"edata": at_x(h)}, device_id_type=MESH)
        pl.semaphore_signal(barrier, inc=1, device_id={"dp": lax.rem(dp + h, NY)}, device_id_type=MESH)

    pltpu.make_async_copy(ids_hbm, ids_s, in_sem.at[0]).start()
    pltpu.make_async_copy(logit_hbm, logit_s, in_sem.at[1]).start()
    for c in range(2):
        for b in range(NY):
            start = pl.multiple_of(owner(b, c) * BLK, BLK)
            pltpu.make_async_copy(
                og_hbm.at[:, pl.ds(start, BLK)],
                og_s.at[pl.ds(c * TOK, TOK), pl.ds(b * BLK, BLK)],
                in_sem.at[2],
            ).start()
    pltpu.make_async_copy(hid_hbm, hid_s, in_sem.at[3]).start()
    for b in range(NY):
        start = pl.multiple_of(owner(b, core) * BLK, BLK)
        pltpu.make_async_copy(
            w_hbm.at[pl.ds(start, BLK)], w_s.at[pl.ds(b * BLK, BLK)], in_sem.at[4]
        ).start()

    pltpu.make_async_copy(ids_hbm, ids_s, in_sem.at[0]).wait()
    pltpu.make_async_copy(logit_hbm, logit_s, in_sem.at[1]).wait()
    ids = ids_s[...]
    scores = jax.nn.sigmoid(logit_s[...])
    score_sum = jnp.sum(scores, axis=0, keepdims=True)
    weights = (2.5 * scores / score_sum).astype(BF).astype(F32)
    rows = NZ * ZROWS
    for part in range(1 + FOLD):
        expert, rank_of = fold_slot(iota((rows, 1), 0), part)
        count, weight, rank = named(ids, weights, expert)
        chosen = jnp.where((count > 0.0) & (rank == rank_of.astype(F32)), weight, 0.0)
        odd = (expert & 1) == 1
        sel_s[pl.ds(part * rows, rows), pl.ds(0, TOK)] = jnp.where(odd, 0.0, chosen).astype(BF)
        sel_s[pl.ds(part * rows, rows), pl.ds(TOK, TOK)] = jnp.where(odd, chosen, 0.0).astype(BF)
    count, _, rank = named(ids, weights, iota((NZ * NJ, 1), 0))
    cnt_s[...] = count
    rank_s[...] = rank

    jr, zrow, rk = slot_parts(iota((SLOTS, 1), 0))
    col = iota((SLOTS, rows), 1)
    same = (col >> 4) == zrow
    s = 3 * jr + rk
    unf_s[:, pl.ds(0, rows)] = (same & ((col & 15) == s)).astype(F32).astype(BF)
    for k in range(FOLD):
        hit = same & ((s >> 2) == k) & ((col & 15) == 12 + (s & 3))
        unf_s[:, pl.ds((k + 1) * rows, rows)] = hit.astype(F32).astype(BF)
    natural = 12 * zrow + 3 * jr + rk
    to_arrival = (iota((SLOTS, SLOTS), 1) == natural).astype(F32).astype(BF)

    for x in range(NX):
        h4[pl.ds(x * PAD + SLOTS, PAD - SLOTS), :] = jnp.zeros((PAD - SLOTS, H), BF)
    pltpu.make_async_copy(hid_hbm, hid_s, in_sem.at[3]).wait()
    mine = pl.ds(pl.multiple_of(ed * PAD, PAD), SLOTS)
    h4[mine, :] = dot(to_arrival, hid_s[...]).astype(BF)
    proj[...] = jnp.zeros_like(proj)
    pltpu.make_async_copy(og_s, og_s, in_sem.at[2]).wait()

    def fold(c):
        cols = pl.multiple_of(c * CH, CH)
        plain = dot(sel_s[pl.ds(0, rows), :], og_s[:, pl.ds(cols, 128 * FOLD)])
        last = og_s[:, pl.ds(pl.multiple_of(cols + 128 * FOLD, 128), 128)]
        for k in range(FOLD):
            part = plain[:, 128 * k : 128 * (k + 1)] + dot(sel_s[pl.ds((k + 1) * rows, rows), :], last)
            zs[c, :, pl.ds(128 * k, 128)] = part.astype(BF)

    z_mine = pl.ds(pl.multiple_of(z * ZROWS, ZROWS), ZROWS)

    def z_send(c):
        for h in OFFS:
            zt = at_z(h)
            theirs = pl.ds(pl.multiple_of(zt * ZROWS, ZROWS), ZROWS)
            remote(zs.at[c, theirs], zr.at[c, z_mine], zs_sem.at[c], zr_sem.at[c], to_z(zt)).start()
        pltpu.make_async_copy(zs.at[c, z_mine], zr.at[c, z_mine], zl_sem.at[c]).start()

    def z_copies(c):
        some = pl.ds(0, (NZ - 1) * ZROWS)
        return remote(zs.at[c, some], zr.at[c, some], zs_sem.at[c], zr_sem.at[c], to_z(z))

    fold(0)
    pl.semaphore_wait(barrier, NZ - 1 + 9)
    z_send(0)
    for h in range(1, NX):
        remote(h4.at[mine], h4.at[mine], hs_sem, hr_sem, {"edata": at_x(h)}).start()

    def first(c, carry):
        fold(c)
        z_send(c)
        return carry

    lax.fori_loop(1, LAG, first, 0)
    pltpu.make_async_copy(w_hbm, w_s, in_sem.at[4]).wait()

    j_mine = pl.ds(pl.multiple_of(j * PLANE_ROWS, PLANE_ROWS), PLANE_ROWS)

    def plane_copies(c):
        cols = pl.ds(pl.multiple_of(c * CH, CH), CH)
        some = pl.ds(0, (NJ - 1) * PLANE_ROWS)
        return remote(ps.at[c, some], ar.at[some, cols], ps_sem.at[c], pr_sem.at[c], to_j(j))

    def chunk(c):
        @pl.when(c + LAG < NCH)
        def _():
            z_copies(c).wait_send()
            fold(c + LAG)
            z_send(c + LAG)

        z_copies(c).wait_recv()
        pltpu.make_async_copy(zs.at[c, z_mine], zr.at[c, z_mine], zl_sem.at[c]).wait()
        ps[c, :, pl.ds(0, 128 * FOLD)] = dot(unf_s[:, pl.ds(0, rows)], zr[c]).astype(BF)
        stacked = jnp.concatenate([zr[c, :, pl.ds(128 * k, 128)] for k in range(FOLD)], axis=0)
        ps[c, :, pl.ds(128 * FOLD, 128)] = dot(unf_s[:, pl.ds(rows, FOLD * rows)], stacked).astype(BF)
        cols = pl.ds(pl.multiple_of(c * CH, CH), CH)
        for h in range(1, NJ):
            jt = at_j(h)
            theirs = pl.ds(pl.multiple_of(jt * PLANE_ROWS, PLANE_ROWS), PLANE_ROWS)
            remote(ps.at[c, theirs], ar.at[j_mine, cols], ps_sem.at[c], pr_sem.at[c], to_j(jt)).start()
        own = pltpu.make_async_copy(ps.at[c, j_mine], ar.at[j_mine, cols], pl_sem.at[c])
        own.start()
        own.wait()
        plane_copies(c).wait_recv()
        proj[...] += dot(ar[:, cols], w_s[cols, :])

    x_mine = pl.ds(pl.multiple_of(ed * PAD, PAD), PAD)

    def block_send(b):
        eye = (iota((128, 128), 0) == iota((128, 128), 1)).astype(F32).astype(BF)
        for g in range(BLK // 128):
            part = ar[:, pl.ds(pl.multiple_of(b * BLK + 128 * g, 128), 128)]
            part = jnp.concatenate([part, jnp.zeros((PAD - SLOTS, 128), BF)], axis=0)
            turned = lax.dot_general(eye, part, (((1,), (1,)), ((), ())), preferred_element_type=F32)
            xs[b, pl.ds(128 * g, 128), :] = turned.astype(BF)
        for h in range(1, NX):
            xt = at_x(h)
            theirs = pl.ds(pl.multiple_of(xt * OWN, 32), OWN)
            remote(xs.at[b, theirs], xr.at[b, :, x_mine], xs_sem.at[b], xr_sem.at[b], {"edata": xt}).start()
        theirs = pl.ds(pl.multiple_of(ed * OWN, 32), OWN)
        pltpu.make_async_copy(xs.at[b, theirs], xr.at[b, :, x_mine], xl_sem.at[b]).start()

    def x_copies(b):
        return remote(
            xs.at[b, pl.ds(0, (NX - 1) * OWN)], xr.at[b, :, pl.ds(0, (NX - 1) * PAD)],
            xs_sem.at[b], xr_sem.at[b], {"edata": ed},
        )

    def block_product(b):
        theirs = pl.ds(pl.multiple_of(ed * OWN, 32), OWN)
        pltpu.make_async_copy(xs.at[b, theirs], xr.at[b, :, x_mine], xl_sem.at[b]).wait()
        x_copies(b).wait_recv()
        return dot(xr[b], h4[...])

    def y_copy(b):
        step = jnp.where(b == 0, 2, jnp.where((b == 1) == (core == 0), 1, 3))
        return remote(ys.at[b], yr.at[b], ys_sem.at[b], yr_sem.at[b], {"dp": lax.rem(dp + step, NY)})

    def h_copies():
        some = pl.ds(0, (NX - 1) * SLOTS)
        return remote(h4.at[some], h4.at[some], hs_sem, hr_sem, {"edata": ed})

    def pair(b, carry):
        chunk(2 * b)
        chunk(2 * b + 1)
        block_send(b)

        @pl.when(b == 0)
        def _():
            h_copies().wait_recv()

        ys[b] = block_product(b).astype(BF)
        y_copy(b).start()
        return carry

    lax.fori_loop(0, NY - 1, pair, 0)
    chunk(NCH - 1)
    block_send(NY - 1)

    total = proj[...]
    slot_grad = jnp.sum(total * h4[mine, :].astype(F32), axis=1, keepdims=True)
    placed = jnp.where(iota((SLOTS, 128), 1) == 3 * j + rk, slot_grad, 0.0)
    gather = (iota((NZ, PLANE_ROWS), 0) == ((iota((NZ, PLANE_ROWS), 1) * 43) >> 7)).astype(F32)
    for jt in range(NJ):
        r1s[jt] = exact_dot(gather, placed[PLANE_ROWS * jt : PLANE_ROWS * (jt + 1)])
    for h in range(1, NJ):
        jt = at_j(h)
        remote(r1s.at[jt], r1r.at[j], r_sem.at[0], r_sem.at[1], to_j(jt)).start()
    r1_own = pltpu.make_async_copy(r1s.at[j], r1r.at[j], r_sem.at[2])
    r1_own.start()

    n = iota((SLOTS, 1), 0)
    nz = (n * 5462) >> 16
    rest = n - 12 * nz
    nj = (rest * 11) >> 5
    to_natural = (iota((SLOTS, SLOTS), 1) == 48 * nj + 3 * nz + (rest - 3 * nj)).astype(F32).astype(BF)
    gh_s[...] = dot(to_natural, total.astype(BF)).astype(BF)
    gh_out = pltpu.make_async_copy(gh_s, gh_hbm, out_sem.at[0])
    gh_out.start()

    r1_own.wait()
    r1_all = remote(r1s.at[pl.ds(0, NJ - 1)], r1r.at[pl.ds(0, NJ - 1)], r_sem.at[0], r_sem.at[1], to_j(j))
    r1_all.wait_recv()
    summed = r1r[0] + r1r[1] + r1r[2] + r1r[3]
    for zt in range(NZ):
        r2s[zt] = jnp.broadcast_to(summed[zt : zt + 1, :], (8, 128))
    for h in OFFS:
        zt = at_z(h)
        remote(r2s.at[zt], r2r.at[z], r_sem.at[3], r_sem.at[4], to_z(zt)).start()
    r2_own = pltpu.make_async_copy(r2s.at[z], r2r.at[z], r_sem.at[5])
    r2_own.start()

    down = block_product(NY - 1)
    for b in range(NY - 1):
        y_copy(b).wait_recv()
        down = down + yr[b].astype(F32)
    gd_s[...] = down.astype(BF)
    gd_out = pltpu.make_async_copy(gd_s, gd_hbm, out_sem.at[1])
    gd_out.start()

    r2_own.wait()
    r2_all = remote(r2s.at[pl.ds(0, NZ - 1)], r2r.at[pl.ds(0, NZ - 1)], r_sem.at[3], r_sem.at[4], to_z(z))
    r2_all.wait_recv()
    planes = jnp.concatenate([r2r[zt, pl.ds(0, 1), :] for zt in range(NZ)], axis=0)
    experts = NZ * NJ
    spread = (iota((experts, NZ), 0) >> 2 == iota((experts, NZ), 1)).astype(F32)
    row = exact_dot(spread, planes)
    e_lane = 3 * (iota((experts, 1), 0) & 3)
    lane = iota((experts, 128), 1)
    grads = jnp.zeros((experts, TOK), F32)
    for r in range(CAP):
        value = jnp.sum(jnp.where(lane == e_lane + r, row, 0.0), axis=1, keepdims=True)
        grads = grads + jnp.where((cnt_s[...] > 0.0) & (rank_s[...] == float(r)), value, 0.0)
    ids = ids_s[...]
    scores = jax.nn.sigmoid(logit_s[...])
    score_sum = jnp.sum(scores, axis=0, keepdims=True)
    weights = (2.5 * scores / score_sum).astype(BF).astype(F32)
    e_col = iota((experts, 1), 0)
    picked = [
        jnp.sum(jnp.where(ids[k : k + 1, :] == e_col, grads, 0.0), axis=0, keepdims=True) for k in range(TOP)
    ]
    combine_grad = jnp.concatenate(picked, axis=0) / weights
    mean = jnp.sum(combine_grad * scores, axis=0, keepdims=True) / score_sum
    lg_s[...] = scores * (1.0 - scores) * (2.5 / score_sum) * (combine_grad - mean)
    lg_out = pltpu.make_async_copy(lg_s, lg_hbm, out_sem.at[2])
    lg_out.start()

    h_copies().wait_send()

    def drain_z(c, carry):
        z_copies(c).wait_send()
        return carry

    def drain_p(c, carry):
        plane_copies(c).wait_send()
        return carry

    def drain_x(b, carry):
        x_copies(b).wait_send()
        return carry

    def drain_y(b, carry):
        y_copy(b).wait_send()
        return carry

    lax.fori_loop(NCH - LAG, NCH, drain_z, 0)
    lax.fori_loop(0, NCH, drain_p, 0)
    lax.fori_loop(0, NY, drain_x, 0)
    lax.fori_loop(0, NY - 1, drain_y, 0)
    r1_all.wait_send()
    r2_all.wait_send()
    gh_out.wait()
    gd_out.wait()
    lg_out.wait()


def on_device(out_grad, route_ids, router_logits, hidden, down_weight):
    rows = NZ * ZROWS
    dma = pltpu.SemaphoreType.DMA
    vm = pltpu.VMEM
    anywhere = pl.BlockSpec(memory_space=pl.ANY)
    grad_down, grad_hidden, logit_grad = pl.pallas_call(
        kernel,
        out_shape=(
            jax.ShapeDtypeStruct((OWN, H), BF),
            jax.ShapeDtypeStruct((SLOTS, H), BF),
            jax.ShapeDtypeStruct((TOP, TOK), F32),
        ),
        in_specs=[anywhere] * 5,
        out_specs=(anywhere,) * 3,
        scratch_shapes=[
            vm((2 * TOK, D), BF), vm((TOP, TOK), jnp.int32), vm((TOP, TOK), F32), vm((SLOTS, H), BF), vm((D, H), BF),
            vm(((1 + FOLD) * rows, 2 * TOK), BF), vm((SLOTS, (1 + FOLD) * rows), BF), vm((NX * PAD, H), BF),
            vm((NCH, rows, 128 * FOLD), BF), vm((NCH, rows, 128 * FOLD), BF), vm((NCH, SLOTS, CH), BF), vm((SLOTS, D), BF),
            vm((NY, BLK, PAD), BF), vm((NY, OWN, NX * PAD), BF), vm((NY - 1, OWN, H), BF), vm((NY - 1, OWN, H), BF),
            vm((SLOTS, H), F32), vm((NZ * NJ, TOK), F32), vm((NZ * NJ, TOK), F32),
            vm((NJ, NZ, 128), F32), vm((NJ, NZ, 128), F32), vm((NZ, 8, 128), F32), vm((NZ, 8, 128), F32),
            vm((OWN, H), BF), vm((SLOTS, H), BF), vm((TOP, TOK), F32),
            dma((5,)), dma((3,)), dma, dma, dma((NCH,)), dma((NCH,)), dma((NCH,)), dma((NCH,)), dma((NCH,)), dma((NCH,)),
            dma((NY,)), dma((NY,)), dma((NY,)), dma((NY - 1,)), dma((NY - 1,)), dma((6,)),
        ],
        compiler_params=pltpu.CompilerParams(
            collective_id=0, has_side_effects=True, vmem_limit_bytes=52 << 20
        ),
        cost_estimate=pl.CostEstimate(flops=4 * SLOTS * D * H, bytes_accessed=2 * D * H, transcendentals=0),
    )(
        out_grad,
        route_ids.T,
        router_logits.T,
        hidden.reshape(SLOTS, H),
        down_weight.reshape(D, H),
    )
    return grad_down.reshape(OWN, 1, H), grad_hidden.reshape(1, 1, SLOTS, H), logit_grad.T


def solution(mesh):
    in_specs = (
        P(("dp", "edata", "expert"), None),
        P(("dp", "edata", "expert"), None),
        P(("dp", "edata", "expert"), None),
        P(("dp", "edata"), "expert", None, None),
        P(None, "expert", None),
    )
    out_specs = (
        P(("dp", "edata"), "expert", None),
        P(("dp", "edata"), "expert", None, None),
        P(("dp", "edata", "expert"), None),
    )
    return jax.shard_map(
        on_device, mesh=mesh, in_specs=in_specs, out_specs=out_specs, check_vma=False
    )
```

time: 348 us -> 152 us (0.44)
  waiting for transfers between devices: 229 us -> 0 us
  Pallas kernels: 0 us -> 147 us
  starting transfers between devices: 35 us -> 0 us
  other arithmetic: 25.4 us -> 0 us
  local copies, waits for them, and re-layouts: 28.8 us -> 4.47 us
  matrix products: 14.2 us -> 0 us
  between operations: 14.2 us -> 0.65 us
    pallas_call x0 -> x1, Pallas kernels: none -> 147 us  [on_device(): pl.pallas_call(kernel, out_shape=(jax.ShapeDtypeStruct((OWN, H), BF), jax...]
    reduce_scatter x1 -> x0, waiting for transfers between devices: 120 us -> none  [on_device(): lax.psum_scatter(jnp.einsum('esd,esj->dej', scaled, local_hidden, preferr...]
    all_to_all x3 -> x0, waiting for transfers between devices: 109 us -> none  [the longest x1 85.8 us: on_device(): lax.all_to_all(send_rows, 'expert', split_axis=0, concat_axis=0, tiled=True)]
    all_to_all x3 -> x0, starting transfers between devices: 34.9 us -> none  [the longest x1 22 us: on_device(): lax.all_to_all(send_rows, 'expert', split_axis=0, concat_axis=0, tiled=True)]
    another operation x2 -> x0, other arithmetic: 18 us -> none
    dot_general x4 -> x0, matrix products: 14.2 us -> none  [the longest x1 7.02 us: on_device(): jnp.einsum('esd,esj->dej', scaled, local_hidden, preferred_element_type=j...]
    gather x3 -> x0, local copies, waits for them, and re-layouts: 13.7 us -> none  [on_device(): picked = jnp.take(returned.reshape(-1), safe_position)]
    convert_element_type x3 -> x0, local copies, waits for them, and re-layouts: 4.09 us -> none  [the longest x1 2.56 us: on_device(): slot_rows.astype(jnp.float32)]
  transfers between devices with their start and end apart: 4 -> 0, of which waited for: 4 -> 0; matrix products, arithmetic and copies ran while one was open for 2% -> 0% of each run, Pallas kernels for 0% -> 0%
where the time goes in v1:
time: 152 us
  Pallas kernels  147 us (97%)
  local copies, waits for them, and re-layouts  4.47 us (3%)
    pallas_call x1, Pallas kernels, on_device(): pl.pallas_call(kernel, out_shape=(jax.ShapeDtypeStruct((OWN, H), BF), jax...  147 us
    unnamed x9, local copies, waits for them, and re-layouts  4.47 us

profile of v1, /device:TPU:1, one launch (start us, length us, event | category | flops | bytes accessed | tf_op | source)
XLA Modules:
  0.0 151.6 jit_solution(10464171945321872484)
XLA Ops:
  0.6 0.0 copy-start
  0.6 1.0 copy-done
  1.6 0.0 copy-start.1
  1.6 0.7 copy-done.1
  2.3 0.0 copy-start.2
  2.3 0.7 copy-done.2
  3.0 146.5 %shard_map.76 = (bf16[224,1024]{1,0:T(8,128)(2,1)S(1)}, bf16[192,1024]{1,0:T(8,128)(2,1)S(1)}, f32[8,128]{1,0:T(8,128)S(1)}) custom-call(bf16[128,3584]{1,0:T(8,128)(2,1)} %og_hbm.1, s32[8,128]{1,0:T(8,128)S(1)} %bitcast.11, f32[8,128]{1,0:T(8,128)S(1)} %bitcast.12, bf16[192,1024]{1,0:T(8,128)(2,1)S(1)} %bitcast.10, bf16[3584,1024]{1,0:T(8,128)(2,1)} %bitcast.13), custom_call_target="tpu_custom_call" | custom-call | flops 2818572288 | bytes 7340032 | tf_op jit(solution)/shard_map/pallas_call | solution.py:399
  149.5 0.8 copy.11
  150.3 0.7 copy.12
  151.1 0.6 copy.13
Async XLA Ops:
  0.6 1.0 copy-start
  1.6 0.7 copy-start.1
  2.3 0.7 copy-start.2

commit v2 on v1

--- a/solution.py
+++ b/solution.py
@@ -26,7 +26,6 @@
 BLK = D // NY
 OWN = BLK // NX
 PAD = 256
-LAG = 3
 OFFS = [8, 7, 9, 6, 10, 5, 11, 4, 12, 3, 13, 2, 14, 1, 15]
 
 
@@ -42,22 +41,26 @@
     return jnp.dot(a, b, preferred_element_type=F32, precision=lax.Precision.HIGHEST)
 
 
-def slot_parts(row):
+def third(q):
+    return (q * 11) >> 5
+
+
+def send_parts(row):
     j = (row * 1366) >> 16
-    rest = row - 48 * j
+    rest = row - PLANE_ROWS * j
     z = (rest * 43) >> 7
     return j, z, rest - 3 * z
 
 
-def fold_slot(row, part):
-    z = row >> 4
+def folded_slot(row, part):
     q = row & 15
     if part == 0:
-        valid, s = q < 12, q
-    else:
-        valid, s = q >= 12, 4 * (part - 1) + (q - 12)
-    j = (s * 11) >> 5
-    return jnp.where(valid, z * NJ + j, -1), s - 3 * j
+        return jnp.where(q < 12, q, -1)
+    return jnp.where(q >= 12, 4 * (part - 1) + (q - 12), -1)
+
+
+def one_hot(mask):
+    return mask.astype(F32).astype(BF)
 
 
 def named(ids, weights, expert):
@@ -76,8 +79,8 @@
 def kernel(
     og_hbm, ids_hbm, logit_hbm, hid_hbm, w_hbm,
     gd_hbm, gh_hbm, lg_hbm,
-    og_s, ids_s, logit_s, hid_s, w_s, sel_s, unf_s, h4, zs, zr, ps, ar, xs, xr, ys, yr, proj,
-    cnt_s, rank_s, r1s, r1r, r2s, r2r, gd_s, gh_s, lg_s,
+    og_s, ids_s, logit_s, w_s, sel_s, fold_s, unf_s, h4, zs, zr, ps, pr, ar, xs, xr, ys, yr, proj,
+    cnt_s, rank_s, r1s, r1r, r2r, gd_s, gh_s, lg_s,
     in_sem, out_sem, hs_sem, hr_sem, zs_sem, zr_sem, zl_sem, ps_sem, pr_sem, pl_sem,
     xs_sem, xr_sem, xl_sem, ys_sem, yr_sem, r_sem,
 ):
@@ -132,7 +135,7 @@
                 og_s.at[pl.ds(c * TOK, TOK), pl.ds(b * BLK, BLK)],
                 in_sem.at[2],
             ).start()
-    pltpu.make_async_copy(hid_hbm, hid_s, in_sem.at[3]).start()
+    pltpu.make_async_copy(hid_hbm, h4.at[pl.ds(pl.multiple_of(ed * PAD, PAD), SLOTS)], in_sem.at[3]).start()
     for b in range(NY):
         start = pl.multiple_of(owner(b, core) * BLK, BLK)
         pltpu.make_async_copy(
@@ -146,99 +149,108 @@
     score_sum = jnp.sum(scores, axis=0, keepdims=True)
     weights = (2.5 * scores / score_sum).astype(BF).astype(F32)
     rows = NZ * ZROWS
+    jt, zt, rank_of = send_parts(iota((SLOTS, 1), 0))
+    count, weight, rank = named(ids, weights, zt * NJ + jt)
+    chosen = jnp.where((count > 0.0) & (rank == rank_of.astype(F32)), weight, 0.0)
+    odd = (jt & 1) == 1
+    sel_s[:, pl.ds(0, TOK)] = jnp.where(odd, 0.0, chosen).astype(BF)
+    sel_s[:, pl.ds(TOK, TOK)] = jnp.where(odd, chosen, 0.0).astype(BF)
+    pltpu.make_async_copy(og_s, og_s, in_sem.at[2]).wait()
+
+    z_mine = pl.ds(pl.multiple_of(z * ZROWS, ZROWS), ZROWS)
+    j_mine = pl.ds(pl.multiple_of(j * PLANE_ROWS, PLANE_ROWS), PLANE_ROWS)
+
+    def select(c):
+        cols = pl.ds(pl.multiple_of(c * CH, CH), CH)
+        ps[c] = dot(sel_s[...], og_s[:, cols]).astype(BF)
+
+    def plane_send(c):
+        for h in range(1, NJ):
+            to = at_j(h)
+            theirs = pl.ds(pl.multiple_of(to * PLANE_ROWS, PLANE_ROWS), PLANE_ROWS)
+            remote(ps.at[c, theirs], pr.at[c, j_mine], ps_sem.at[c], pr_sem.at[c], to_j(to)).start()
+        pltpu.make_async_copy(ps.at[c, j_mine], pr.at[c, j_mine], pl_sem.at[c]).start()
+
+    def plane_copies(c):
+        some = pl.ds(0, (NJ - 1) * PLANE_ROWS)
+        return remote(ps.at[c, some], pr.at[c, some], ps_sem.at[c], pr_sem.at[c], to_j(j))
+
+    def fold(c):
+        plain = dot(fold_s[pl.ds(0, rows), :], pr[c, :, pl.ds(0, 128 * FOLD)])
+        last = dot(fold_s[pl.ds(rows, FOLD * rows), :], pr[c, :, pl.ds(128 * FOLD, 128)])
+        for k in range(FOLD):
+            part = plain[:, 128 * k : 128 * (k + 1)] + last[rows * k : rows * (k + 1)]
+            zs[c, :, pl.ds(128 * k, 128)] = part.astype(BF)
+
+    def z_send(c):
+        for h in OFFS:
+            to = at_z(h)
+            theirs = pl.ds(pl.multiple_of(to * ZROWS, ZROWS), ZROWS)
+            remote(zs.at[c, theirs], zr.at[c, z_mine], zs_sem.at[c], zr_sem.at[c], to_z(to)).start()
+        pltpu.make_async_copy(zs.at[c, z_mine], zr.at[c, z_mine], zl_sem.at[c]).start()
+
+    def z_copies(c):
+        some = pl.ds(0, (NZ - 1) * ZROWS)
+        return remote(zs.at[c, some], zr.at[c, some], zs_sem.at[c], zr_sem.at[c], to_z(z))
+
+    def select_loop(c, carry):
+        select(c)
+        return carry
+
+    lax.fori_loop(0, NCH, select_loop, 0)
+
+    row = iota((rows, 1), 0)
+    cj, cz, crank = send_parts(iota((rows, SLOTS), 1))
     for part in range(1 + FOLD):
-        expert, rank_of = fold_slot(iota((rows, 1), 0), part)
-        count, weight, rank = named(ids, weights, expert)
-        chosen = jnp.where((count > 0.0) & (rank == rank_of.astype(F32)), weight, 0.0)
-        odd = (expert & 1) == 1
-        sel_s[pl.ds(part * rows, rows), pl.ds(0, TOK)] = jnp.where(odd, 0.0, chosen).astype(BF)
-        sel_s[pl.ds(part * rows, rows), pl.ds(TOK, TOK)] = jnp.where(odd, chosen, 0.0).astype(BF)
+        slot = folded_slot(row, part)
+        fold_s[pl.ds(part * rows, rows), :] = one_hot((cz == (row >> 4)) & (3 * cj + crank == slot))
+    n = iota((SLOTS, 1), 0)
+    nz = (n * 5462) >> 16
+    col = iota((SLOTS, rows), 1)
+    for part in range(1 + FOLD):
+        slot = folded_slot(col, part)
+        unf_s[:, pl.ds(part * rows, rows)] = one_hot(((col >> 4) == nz) & (n - 12 * nz == slot))
+
+    for x in range(NX):
+        h4[pl.ds(x * PAD + SLOTS, PAD - SLOTS), :] = jnp.zeros((PAD - SLOTS, H), BF)
+    mine = pl.ds(pl.multiple_of(ed * PAD, PAD), SLOTS)
+    pltpu.make_async_copy(hid_hbm, h4.at[mine], in_sem.at[3]).wait()
+    proj[...] = jnp.zeros_like(proj)
     count, _, rank = named(ids, weights, iota((NZ * NJ, 1), 0))
     cnt_s[...] = count
     rank_s[...] = rank
 
-    jr, zrow, rk = slot_parts(iota((SLOTS, 1), 0))
-    col = iota((SLOTS, rows), 1)
-    same = (col >> 4) == zrow
-    s = 3 * jr + rk
-    unf_s[:, pl.ds(0, rows)] = (same & ((col & 15) == s)).astype(F32).astype(BF)
-    for k in range(FOLD):
-        hit = same & ((s >> 2) == k) & ((col & 15) == 12 + (s & 3))
-        unf_s[:, pl.ds((k + 1) * rows, rows)] = hit.astype(F32).astype(BF)
-    natural = 12 * zrow + 3 * jr + rk
-    to_arrival = (iota((SLOTS, SLOTS), 1) == natural).astype(F32).astype(BF)
-
-    for x in range(NX):
-        h4[pl.ds(x * PAD + SLOTS, PAD - SLOTS), :] = jnp.zeros((PAD - SLOTS, H), BF)
-    pltpu.make_async_copy(hid_hbm, hid_s, in_sem.at[3]).wait()
-    mine = pl.ds(pl.multiple_of(ed * PAD, PAD), SLOTS)
-    h4[mine, :] = dot(to_arrival, hid_s[...]).astype(BF)
-    proj[...] = jnp.zeros_like(proj)
-    pltpu.make_async_copy(og_s, og_s, in_sem.at[2]).wait()
-
-    def fold(c):
-        cols = pl.multiple_of(c * CH, CH)
-        plain = dot(sel_s[pl.ds(0, rows), :], og_s[:, pl.ds(cols, 128 * FOLD)])
-        last = og_s[:, pl.ds(pl.multiple_of(cols + 128 * FOLD, 128), 128)]
-        for k in range(FOLD):
-            part = plain[:, 128 * k : 128 * (k + 1)] + dot(sel_s[pl.ds((k + 1) * rows, rows), :], last)
-            zs[c, :, pl.ds(128 * k, 128)] = part.astype(BF)
-
-    z_mine = pl.ds(pl.multiple_of(z * ZROWS, ZROWS), ZROWS)
-
-    def z_send(c):
-        for h in OFFS:
-            zt = at_z(h)
-            theirs = pl.ds(pl.multiple_of(zt * ZROWS, ZROWS), ZROWS)
-            remote(zs.at[c, theirs], zr.at[c, z_mine], zs_sem.at[c], zr_sem.at[c], to_z(zt)).start()
-        pltpu.make_async_copy(zs.at[c, z_mine], zr.at[c, z_mine], zl_sem.at[c]).start()
-
-    def z_copies(c):
-        some = pl.ds(0, (NZ - 1) * ZROWS)
-        return remote(zs.at[c, some], zr.at[c, some], zs_sem.at[c], zr_sem.at[c], to_z(z))
-
-    fold(0)
     pl.semaphore_wait(barrier, NZ - 1 + 9)
-    z_send(0)
+
+    def plane_loop(c, carry):
+        plane_send(c)
+        return carry
+
+    lax.fori_loop(0, NCH, plane_loop, 0)
     for h in range(1, NX):
         remote(h4.at[mine], h4.at[mine], hs_sem, hr_sem, {"edata": at_x(h)}).start()
 
-    def first(c, carry):
+    def fold_loop(c, carry):
+        pltpu.make_async_copy(ps.at[c, j_mine], pr.at[c, j_mine], pl_sem.at[c]).wait()
+        plane_copies(c).wait_recv()
         fold(c)
         z_send(c)
         return carry
 
-    lax.fori_loop(1, LAG, first, 0)
+    lax.fori_loop(0, NCH, fold_loop, 0)
     pltpu.make_async_copy(w_hbm, w_s, in_sem.at[4]).wait()
 
-    j_mine = pl.ds(pl.multiple_of(j * PLANE_ROWS, PLANE_ROWS), PLANE_ROWS)
-
-    def plane_copies(c):
-        cols = pl.ds(pl.multiple_of(c * CH, CH), CH)
-        some = pl.ds(0, (NJ - 1) * PLANE_ROWS)
-        return remote(ps.at[c, some], ar.at[some, cols], ps_sem.at[c], pr_sem.at[c], to_j(j))
-
     def chunk(c):
-        @pl.when(c + LAG < NCH)
-        def _():
-            z_copies(c).wait_send()
-            fold(c + LAG)
-            z_send(c + LAG)
-
         z_copies(c).wait_recv()
         pltpu.make_async_copy(zs.at[c, z_mine], zr.at[c, z_mine], zl_sem.at[c]).wait()
-        ps[c, :, pl.ds(0, 128 * FOLD)] = dot(unf_s[:, pl.ds(0, rows)], zr[c]).astype(BF)
+        first = pl.multiple_of(c * CH, CH)
+        ar[:, pl.ds(first, 128 * FOLD)] = dot(unf_s[:, pl.ds(0, rows)], zr[c]).astype(BF)
         stacked = jnp.concatenate([zr[c, :, pl.ds(128 * k, 128)] for k in range(FOLD)], axis=0)
-        ps[c, :, pl.ds(128 * FOLD, 128)] = dot(unf_s[:, pl.ds(rows, FOLD * rows)], stacked).astype(BF)
+        last = pl.ds(pl.multiple_of(first + 128 * FOLD, 128), 128)
+        ar[:, last] = dot(unf_s[:, pl.ds(rows, FOLD * rows)], stacked).astype(BF)
+
+    def project(c):
         cols = pl.ds(pl.multiple_of(c * CH, CH), CH)
-        for h in range(1, NJ):
-            jt = at_j(h)
-            theirs = pl.ds(pl.multiple_of(jt * PLANE_ROWS, PLANE_ROWS), PLANE_ROWS)
-            remote(ps.at[c, theirs], ar.at[j_mine, cols], ps_sem.at[c], pr_sem.at[c], to_j(jt)).start()
-        own = pltpu.make_async_copy(ps.at[c, j_mine], ar.at[j_mine, cols], pl_sem.at[c])
-        own.start()
-        own.wait()
-        plane_copies(c).wait_recv()
         proj[...] += dot(ar[:, cols], w_s[cols, :])
 
     x_mine = pl.ds(pl.multiple_of(ed * PAD, PAD), PAD)
@@ -279,8 +291,10 @@
 
     def pair(b, carry):
         chunk(2 * b)
+        project(2 * b)
         chunk(2 * b + 1)
         block_send(b)
+        project(2 * b + 1)
 
         @pl.when(b == 0)
         def _():
@@ -293,39 +307,31 @@
     lax.fori_loop(0, NY - 1, pair, 0)
     chunk(NCH - 1)
     block_send(NY - 1)
+    project(NCH - 1)
 
     total = proj[...]
     slot_grad = jnp.sum(total * h4[mine, :].astype(F32), axis=1, keepdims=True)
-    placed = jnp.where(iota((SLOTS, 128), 1) == 3 * j + rk, slot_grad, 0.0)
-    gather = (iota((NZ, PLANE_ROWS), 0) == ((iota((NZ, PLANE_ROWS), 1) * 43) >> 7)).astype(F32)
-    for jt in range(NJ):
-        r1s[jt] = exact_dot(gather, placed[PLANE_ROWS * jt : PLANE_ROWS * (jt + 1)])
-    for h in range(1, NJ):
-        jt = at_j(h)
-        remote(r1s.at[jt], r1r.at[j], r_sem.at[0], r_sem.at[1], to_j(jt)).start()
-    r1_own = pltpu.make_async_copy(r1s.at[j], r1r.at[j], r_sem.at[2])
+    placed = jnp.where(iota((SLOTS, 128), 1) == n - 12 * nz, slot_grad, 0.0)
+    gather = (iota((NZ, SLOTS), 0) == ((iota((NZ, SLOTS), 1) * 5462) >> 16)).astype(F32)
+    by_plane = exact_dot(gather, placed)
+    for to in range(NZ):
+        r1s[to] = jnp.broadcast_to(by_plane[to : to + 1, :], (8, 128))
+    for h in OFFS:
+        to = at_z(h)
+        remote(r1s.at[to], r1r.at[z], r_sem.at[0], r_sem.at[1], to_z(to)).start()
+    r1_own = pltpu.make_async_copy(r1s.at[z], r1r.at[z], r_sem.at[2])
     r1_own.start()
-
-    n = iota((SLOTS, 1), 0)
-    nz = (n * 5462) >> 16
-    rest = n - 12 * nz
-    nj = (rest * 11) >> 5
-    to_natural = (iota((SLOTS, SLOTS), 1) == 48 * nj + 3 * nz + (rest - 3 * nj)).astype(F32).astype(BF)
-    gh_s[...] = dot(to_natural, total.astype(BF)).astype(BF)
+    gh_s[...] = total.astype(BF)
     gh_out = pltpu.make_async_copy(gh_s, gh_hbm, out_sem.at[0])
     gh_out.start()
-
     r1_own.wait()
-    r1_all = remote(r1s.at[pl.ds(0, NJ - 1)], r1r.at[pl.ds(0, NJ - 1)], r_sem.at[0], r_sem.at[1], to_j(j))
+    r1_all = remote(r1s.at[pl.ds(0, NZ - 1)], r1r.at[pl.ds(0, NZ - 1)], r_sem.at[0], r_sem.at[1], to_z(z))
     r1_all.wait_recv()
-    summed = r1r[0] + r1r[1] + r1r[2] + r1r[3]
-    for zt in range(NZ):
-        r2s[zt] = jnp.broadcast_to(summed[zt : zt + 1, :], (8, 128))
-    for h in OFFS:
-        zt = at_z(h)
-        remote(r2s.at[zt], r2r.at[z], r_sem.at[3], r_sem.at[4], to_z(zt)).start()
-    r2_own = pltpu.make_async_copy(r2s.at[z], r2r.at[z], r_sem.at[5])
-    r2_own.start()
+    planes = jnp.concatenate([r1r[zt, pl.ds(0, 1), :] for zt in range(NZ)], axis=0)
+    j_rows = pl.ds(pl.multiple_of(j * NZ, NZ), NZ)
+    r2r[j_rows, :] = planes
+    for h in range(1, NJ):
+        remote(r2r.at[j_rows], r2r.at[j_rows], r_sem.at[3], r_sem.at[4], to_j(at_j(h))).start()
 
     down = block_product(NY - 1)
     for b in range(NY - 1):
@@ -335,18 +341,17 @@
     gd_out = pltpu.make_async_copy(gd_s, gd_hbm, out_sem.at[1])
     gd_out.start()
 
-    r2_own.wait()
-    r2_all = remote(r2s.at[pl.ds(0, NZ - 1)], r2r.at[pl.ds(0, NZ - 1)], r_sem.at[3], r_sem.at[4], to_z(z))
+    some = pl.ds(0, (NJ - 1) * NZ)
+    r2_all = remote(r2r.at[some], r2r.at[some], r_sem.at[3], r_sem.at[4], to_j(j))
     r2_all.wait_recv()
-    planes = jnp.concatenate([r2r[zt, pl.ds(0, 1), :] for zt in range(NZ)], axis=0)
     experts = NZ * NJ
-    spread = (iota((experts, NZ), 0) >> 2 == iota((experts, NZ), 1)).astype(F32)
-    row = exact_dot(spread, planes)
-    e_lane = 3 * (iota((experts, 1), 0) & 3)
-    lane = iota((experts, 128), 1)
+    e_row = iota((experts, experts), 0)
+    spread = (iota((experts, experts), 1) == (e_row & 3) * NZ + (e_row >> 2)).astype(F32)
+    values = exact_dot(spread, r2r[...])
+    lane = iota((experts, 128), 1) - 3 * j
     grads = jnp.zeros((experts, TOK), F32)
     for r in range(CAP):
-        value = jnp.sum(jnp.where(lane == e_lane + r, row, 0.0), axis=1, keepdims=True)
+        value = jnp.sum(jnp.where(lane == r, values, 0.0), axis=1, keepdims=True)
         grads = grads + jnp.where((cnt_s[...] > 0.0) & (rank_s[...] == float(r)), value, 0.0)
     ids = ids_s[...]
     scores = jax.nn.sigmoid(logit_s[...])
@@ -380,7 +385,7 @@
         y_copy(b).wait_send()
         return carry
 
-    lax.fori_loop(NCH - LAG, NCH, drain_z, 0)
+    lax.fori_loop(0, NCH, drain_z, 0)
     lax.fori_loop(0, NCH, drain_p, 0)
     lax.fori_loop(0, NY, drain_x, 0)
     lax.fori_loop(0, NY - 1, drain_y, 0)
@@ -406,18 +411,18 @@
         in_specs=[anywhere] * 5,
         out_specs=(anywhere,) * 3,
         scratch_shapes=[
-            vm((2 * TOK, D), BF), vm((TOP, TOK), jnp.int32), vm((TOP, TOK), F32), vm((SLOTS, H), BF), vm((D, H), BF),
-            vm(((1 + FOLD) * rows, 2 * TOK), BF), vm((SLOTS, (1 + FOLD) * rows), BF), vm((NX * PAD, H), BF),
-            vm((NCH, rows, 128 * FOLD), BF), vm((NCH, rows, 128 * FOLD), BF), vm((NCH, SLOTS, CH), BF), vm((SLOTS, D), BF),
+            vm((2 * TOK, D), BF), vm((TOP, TOK), jnp.int32), vm((TOP, TOK), F32), vm((D, H), BF),
+            vm((SLOTS, 2 * TOK), BF), vm(((1 + FOLD) * rows, SLOTS), BF), vm((SLOTS, (1 + FOLD) * rows), BF), vm((NX * PAD, H), BF),
+            vm((NCH, rows, 128 * FOLD), BF), vm((NCH, rows, 128 * FOLD), BF), vm((NCH, SLOTS, CH), BF), vm((NCH, SLOTS, CH), BF), vm((SLOTS, D), BF),
             vm((NY, BLK, PAD), BF), vm((NY, OWN, NX * PAD), BF), vm((NY - 1, OWN, H), BF), vm((NY - 1, OWN, H), BF),
             vm((SLOTS, H), F32), vm((NZ * NJ, TOK), F32), vm((NZ * NJ, TOK), F32),
-            vm((NJ, NZ, 128), F32), vm((NJ, NZ, 128), F32), vm((NZ, 8, 128), F32), vm((NZ, 8, 128), F32),
+            vm((NZ, 8, 128), F32), vm((NZ, 8, 128), F32), vm((NJ * NZ, 128), F32),
             vm((OWN, H), BF), vm((SLOTS, H), BF), vm((TOP, TOK), F32),
             dma((5,)), dma((3,)), dma, dma, dma((NCH,)), dma((NCH,)), dma((NCH,)), dma((NCH,)), dma((NCH,)), dma((NCH,)),
             dma((NY,)), dma((NY,)), dma((NY,)), dma((NY - 1,)), dma((NY - 1,)), dma((6,)),
         ],
         compiler_params=pltpu.CompilerParams(
-            collective_id=0, has_side_effects=True, vmem_limit_bytes=52 << 20
+            collective_id=0, has_side_effects=True, vmem_limit_bytes=62 << 20
         ),
         cost_estimate=pl.CostEstimate(flops=4 * SLOTS * D * H, bytes_accessed=2 * D * H, transcendentals=0),
     )(

time: 152 us -> 112 us (0.74)
  Pallas kernels: 147 us -> 106 us
    pallas_call x1, Pallas kernels: 147 us -> 106 us  [on_device(): pl.pallas_call(kernel, out_shape=(jax.ShapeDtypeStruct((OWN, H), BF), jax...]
    unnamed x9 -> x3, local copies, waits for them, and re-layouts: 4.47 us -> 4.86 us
where the time goes in v2:
time: 112 us
  Pallas kernels  106 us (95%)
  local copies, waits for them, and re-layouts  4.86 us (4%)
    pallas_call x1, Pallas kernels, on_device(): pl.pallas_call(kernel, out_shape=(jax.ShapeDtypeStruct((OWN, H), BF), jax...  106 us
    unnamed x3, local copies, waits for them, and re-layouts  4.86 us

profile of v2, /device:TPU:1, one launch (start us, length us, event | category | flops | bytes accessed | tf_op | source)
XLA Modules:
  0.0 111.7 jit_solution(6548047852503979397)
XLA Ops:
  0.6 106.2 %shard_map.76 = (bf16[224,1024]{1,0:T(8,128)(2,1)}, bf16[192,1024]{1,0:T(8,128)(2,1)}, f32[8,128]{1,0:T(8,128)}) custom-call(bf16[128,3584]{1,0:T(8,128)(2,1)} %og_hbm.1, s32[8,128]{1,0:T(8,128)} %bitcast.12, f32[8,128]{1,0:T(8,128)} %bitcast.13, bf16[192,1024]{1,0:T(8,128)(2,1)} %bitcast.11, bf16[3584,1024]{1,0:T(8,128)(2,1)} %bitcast.10), custom_call_target="tpu_custom_call" | custom-call | flops 2818572288 | bytes 7340032 | tf_op jit(solution)/shard_map/pallas_call | solution.py:404
  106.8 1.8 %copy.11 = bf16[224,1,1024]{2,0,1:T(8,128)(2,1)} copy(bf16[224,1,1024]{2,0,1:T(8,128)(2,1)} %bitcast.7) | data formatting | bytes 917504
  108.6 1.8 %copy.12 = bf16[1,1,192,1024]{3,2,1,0:T(8,128)(2,1)} copy(bf16[1,1,192,1024]{3,2,1,0:T(8,128)(2,1)} %bitcast.8) | data formatting | bytes 786432
  110.4 1.3 %copy.13 = f32[128,8]{0,1:T(8,128)} copy(f32[128,8]{0,1:T(8,128)} %bitcast.9) | data formatting | bytes 8192

commit v3 on v2

--- a/solution.py
+++ b/solution.py
@@ -26,6 +26,7 @@
 BLK = D // NY
 OWN = BLK // NX
 PAD = 256
+SPLIT = (BLK * (NY - 1)) // CH
 OFFS = [8, 7, 9, 6, 10, 5, 11, 4, 12, 3, 13, 2, 14, 1, 15]
 
 
@@ -182,28 +183,66 @@
             part = plain[:, 128 * k : 128 * (k + 1)] + last[rows * k : rows * (k + 1)]
             zs[c, :, pl.ds(128 * k, 128)] = part.astype(BF)
 
-    def z_send(c):
+    def z_send(c, first=0, width=128 * FOLD, at=None):
+        at = c if at is None else at
+        part = pl.ds(first, width)
         for h in OFFS:
             to = at_z(h)
             theirs = pl.ds(pl.multiple_of(to * ZROWS, ZROWS), ZROWS)
-            remote(zs.at[c, theirs], zr.at[c, z_mine], zs_sem.at[c], zr_sem.at[c], to_z(to)).start()
-        pltpu.make_async_copy(zs.at[c, z_mine], zr.at[c, z_mine], zl_sem.at[c]).start()
-
-    def z_copies(c):
-        some = pl.ds(0, (NZ - 1) * ZROWS)
-        return remote(zs.at[c, some], zr.at[c, some], zs_sem.at[c], zr_sem.at[c], to_z(z))
-
-    def select_loop(c, carry):
-        select(c)
-        return carry
-
-    lax.fori_loop(0, NCH, select_loop, 0)
+            remote(
+                zs.at[c, theirs, part], zr.at[c, z_mine, part], zs_sem.at[at], zr_sem.at[at], to_z(to)
+            ).start()
+
+    def z_own(c):
+        return pltpu.make_async_copy(zs.at[c, z_mine], zr.at[c, z_mine], zl_sem.at[c])
+
+    def z_copies(c, first=0, width=128 * FOLD, at=None):
+        at = c if at is None else at
+        some, part = pl.ds(0, (NZ - 1) * ZROWS), pl.ds(first, width)
+        return remote(zs.at[c, some, part], zr.at[c, some, part], zs_sem.at[at], zr_sem.at[at], to_z(z))
+
+    select(0)
+    pl.semaphore_wait(barrier, NZ - 1 + 9)
+    plane_send(0)
+    select(1)
+    plane_send(1)
 
     row = iota((rows, 1), 0)
     cj, cz, crank = send_parts(iota((rows, SLOTS), 1))
     for part in range(1 + FOLD):
         slot = folded_slot(row, part)
         fold_s[pl.ds(part * rows, rows), :] = one_hot((cz == (row >> 4)) & (3 * cj + crank == slot))
+    def fold_and_send(c):
+        pltpu.make_async_copy(ps.at[c, j_mine], pr.at[c, j_mine], pl_sem.at[c]).wait()
+        plane_copies(c).wait_recv()
+        fold(c)
+        z_own(c).start()
+
+    fold_and_send(0)
+    z_send(0)
+    mine = pl.ds(pl.multiple_of(ed * PAD, PAD), SLOTS)
+    pltpu.make_async_copy(hid_hbm, h4.at[mine], in_sem.at[3]).wait()
+    for h in range(1, NX):
+        remote(h4.at[mine], h4.at[mine], hs_sem, hr_sem, {"edata": at_x(h)}).start()
+
+    def fold_loop(c, carry):
+        select(c + 1)
+        plane_send(c + 1)
+        fold_and_send(c)
+        z_send(c)
+        return carry
+
+    lax.fori_loop(1, SPLIT, fold_loop, 0)
+    for c in range(SPLIT + 1, NCH):
+        select(c)
+        plane_send(c)
+    fold_and_send(SPLIT)
+    z_send(SPLIT, 0, 128, NCH)
+    z_send(SPLIT, 128, 128 * (FOLD - 1))
+    for c in range(SPLIT + 1, NCH):
+        fold_and_send(c)
+        z_send(c)
+
     n = iota((SLOTS, 1), 0)
     nz = (n * 5462) >> 16
     col = iota((SLOTS, rows), 1)
@@ -213,41 +252,33 @@
 
     for x in range(NX):
         h4[pl.ds(x * PAD + SLOTS, PAD - SLOTS), :] = jnp.zeros((PAD - SLOTS, H), BF)
-    mine = pl.ds(pl.multiple_of(ed * PAD, PAD), SLOTS)
-    pltpu.make_async_copy(hid_hbm, h4.at[mine], in_sem.at[3]).wait()
     proj[...] = jnp.zeros_like(proj)
     count, _, rank = named(ids, weights, iota((NZ * NJ, 1), 0))
     cnt_s[...] = count
     rank_s[...] = rank
 
-    pl.semaphore_wait(barrier, NZ - 1 + 9)
-
-    def plane_loop(c, carry):
-        plane_send(c)
-        return carry
-
-    lax.fori_loop(0, NCH, plane_loop, 0)
-    for h in range(1, NX):
-        remote(h4.at[mine], h4.at[mine], hs_sem, hr_sem, {"edata": at_x(h)}).start()
-
-    def fold_loop(c, carry):
-        pltpu.make_async_copy(ps.at[c, j_mine], pr.at[c, j_mine], pl_sem.at[c]).wait()
-        plane_copies(c).wait_recv()
-        fold(c)
-        z_send(c)
-        return carry
-
-    lax.fori_loop(0, NCH, fold_loop, 0)
     pltpu.make_async_copy(w_hbm, w_s, in_sem.at[4]).wait()
+
+    eye = one_hot(iota((128, 128), 0) == iota((128, 128), 1))
+
+    def turn(group):
+        cols = pl.ds(pl.multiple_of(group * 128, 128), 128)
+        part = jnp.concatenate([ar[:, cols], jnp.zeros((PAD - SLOTS, 128), BF)], axis=0)
+        turned = lax.dot_general(eye, part, (((1,), (1,)), ((), ())), preferred_element_type=F32)
+        xs[cols, :] = turned.astype(BF)
+
+    def unfold_last(c):
+        stacked = jnp.concatenate([zr[c, :, pl.ds(128 * k, 128)] for k in range(FOLD)], axis=0)
+        last = pl.ds(pl.multiple_of(c * CH + 128 * FOLD, 128), 128)
+        ar[:, last] = dot(unf_s[:, pl.ds(rows, FOLD * rows)], stacked).astype(BF)
 
     def chunk(c):
         z_copies(c).wait_recv()
-        pltpu.make_async_copy(zs.at[c, z_mine], zr.at[c, z_mine], zl_sem.at[c]).wait()
-        first = pl.multiple_of(c * CH, CH)
-        ar[:, pl.ds(first, 128 * FOLD)] = dot(unf_s[:, pl.ds(0, rows)], zr[c]).astype(BF)
-        stacked = jnp.concatenate([zr[c, :, pl.ds(128 * k, 128)] for k in range(FOLD)], axis=0)
-        last = pl.ds(pl.multiple_of(first + 128 * FOLD, 128), 128)
-        ar[:, last] = dot(unf_s[:, pl.ds(rows, FOLD * rows)], stacked).astype(BF)
+        z_own(c).wait()
+        ar[:, pl.ds(pl.multiple_of(c * CH, CH), 128 * FOLD)] = dot(unf_s[:, pl.ds(0, rows)], zr[c]).astype(BF)
+        unfold_last(c)
+        for g in range(FOLD + 1):
+            turn(c * (FOLD + 1) + g)
 
     def project(c):
         cols = pl.ds(pl.multiple_of(c * CH, CH), CH)
@@ -255,29 +286,25 @@
 
     x_mine = pl.ds(pl.multiple_of(ed * PAD, PAD), PAD)
 
+    def x_own(b):
+        ours = pl.ds(pl.multiple_of(b * BLK + ed * OWN, 32), OWN)
+        return pltpu.make_async_copy(xs.at[ours], xr.at[b, :, x_mine], xl_sem.at[b])
+
     def block_send(b):
-        eye = (iota((128, 128), 0) == iota((128, 128), 1)).astype(F32).astype(BF)
-        for g in range(BLK // 128):
-            part = ar[:, pl.ds(pl.multiple_of(b * BLK + 128 * g, 128), 128)]
-            part = jnp.concatenate([part, jnp.zeros((PAD - SLOTS, 128), BF)], axis=0)
-            turned = lax.dot_general(eye, part, (((1,), (1,)), ((), ())), preferred_element_type=F32)
-            xs[b, pl.ds(128 * g, 128), :] = turned.astype(BF)
         for h in range(1, NX):
             xt = at_x(h)
-            theirs = pl.ds(pl.multiple_of(xt * OWN, 32), OWN)
-            remote(xs.at[b, theirs], xr.at[b, :, x_mine], xs_sem.at[b], xr_sem.at[b], {"edata": xt}).start()
-        theirs = pl.ds(pl.multiple_of(ed * OWN, 32), OWN)
-        pltpu.make_async_copy(xs.at[b, theirs], xr.at[b, :, x_mine], xl_sem.at[b]).start()
+            theirs = pl.ds(pl.multiple_of(b * BLK + xt * OWN, 32), OWN)
+            remote(xs.at[theirs], xr.at[b, :, x_mine], xs_sem.at[b], xr_sem.at[b], {"edata": xt}).start()
+        x_own(b).start()
 
     def x_copies(b):
         return remote(
-            xs.at[b, pl.ds(0, (NX - 1) * OWN)], xr.at[b, :, pl.ds(0, (NX - 1) * PAD)],
+            xs.at[pl.ds(0, (NX - 1) * OWN)], xr.at[b, :, pl.ds(0, (NX - 1) * PAD)],
             xs_sem.at[b], xr_sem.at[b], {"edata": ed},
         )
 
     def block_product(b):
-        theirs = pl.ds(pl.multiple_of(ed * OWN, 32), OWN)
-        pltpu.make_async_copy(xs.at[b, theirs], xr.at[b, :, x_mine], xl_sem.at[b]).wait()
+        x_own(b).wait()
         x_copies(b).wait_recv()
         return dot(xr[b], h4[...])
 
@@ -304,7 +331,23 @@
         y_copy(b).start()
         return carry
 
-    lax.fori_loop(0, NY - 1, pair, 0)
+    lax.fori_loop(0, NY - 2, pair, 0)
+    chunk(SPLIT - 1)
+    project(SPLIT - 1)
+    z_copies(SPLIT, 0, 128, NCH).wait_recv()
+    z_own(SPLIT).wait()
+    ar[:, pl.ds(SPLIT * CH, 128)] = dot(unf_s[:, pl.ds(0, rows)], zr[SPLIT, :, pl.ds(0, 128)]).astype(BF)
+    turn(SPLIT * (FOLD + 1))
+    block_send(NY - 2)
+    z_copies(SPLIT, 128, 128 * (FOLD - 1)).wait_recv()
+    rest = zr[SPLIT, :, pl.ds(128, 128 * (FOLD - 1))]
+    ar[:, pl.ds(SPLIT * CH + 128, 128 * (FOLD - 1))] = dot(unf_s[:, pl.ds(0, rows)], rest).astype(BF)
+    unfold_last(SPLIT)
+    for g in range(1, FOLD + 1):
+        turn(SPLIT * (FOLD + 1) + g)
+    project(SPLIT)
+    ys[NY - 2] = block_product(NY - 2).astype(BF)
+    y_copy(NY - 2).start()
     chunk(NCH - 1)
     block_send(NY - 1)
     project(NCH - 1)
@@ -385,7 +428,10 @@
         y_copy(b).wait_send()
         return carry
 
-    lax.fori_loop(0, NCH, drain_z, 0)
+    lax.fori_loop(0, SPLIT, drain_z, 0)
+    z_copies(SPLIT, 0, 128, NCH).wait_send()
+    z_copies(SPLIT, 128, 128 * (FOLD - 1)).wait_send()
+    lax.fori_loop(SPLIT + 1, NCH, drain_z, 0)
     lax.fori_loop(0, NCH, drain_p, 0)
     lax.fori_loop(0, NY, drain_x, 0)
     lax.fori_loop(0, NY - 1, drain_y, 0)
@@ -408,21 +454,21 @@
             jax.ShapeDtypeStruct((SLOTS, H), BF),
             jax.ShapeDtypeStruct((TOP, TOK), F32),
         ),
-        in_specs=[anywhere] * 5,
+        in_specs=[pl.BlockSpec(memory_space=pltpu.HBM)] * 5,
         out_specs=(anywhere,) * 3,
         scratch_shapes=[
             vm((2 * TOK, D), BF), vm((TOP, TOK), jnp.int32), vm((TOP, TOK), F32), vm((D, H), BF),
             vm((SLOTS, 2 * TOK), BF), vm(((1 + FOLD) * rows, SLOTS), BF), vm((SLOTS, (1 + FOLD) * rows), BF), vm((NX * PAD, H), BF),
             vm((NCH, rows, 128 * FOLD), BF), vm((NCH, rows, 128 * FOLD), BF), vm((NCH, SLOTS, CH), BF), vm((NCH, SLOTS, CH), BF), vm((SLOTS, D), BF),
-            vm((NY, BLK, PAD), BF), vm((NY, OWN, NX * PAD), BF), vm((NY - 1, OWN, H), BF), vm((NY - 1, OWN, H), BF),
+            vm((D, PAD), BF), vm((NY, OWN, NX * PAD), BF), vm((NY - 1, OWN, H), BF), vm((NY - 1, OWN, H), BF),
             vm((SLOTS, H), F32), vm((NZ * NJ, TOK), F32), vm((NZ * NJ, TOK), F32),
             vm((NZ, 8, 128), F32), vm((NZ, 8, 128), F32), vm((NJ * NZ, 128), F32),
             vm((OWN, H), BF), vm((SLOTS, H), BF), vm((TOP, TOK), F32),
-            dma((5,)), dma((3,)), dma, dma, dma((NCH,)), dma((NCH,)), dma((NCH,)), dma((NCH,)), dma((NCH,)), dma((NCH,)),
+            dma((5,)), dma((3,)), dma, dma, dma((NCH + 1,)), dma((NCH + 1,)), dma((NCH,)), dma((NCH,)), dma((NCH,)), dma((NCH,)),
             dma((NY,)), dma((NY,)), dma((NY,)), dma((NY - 1,)), dma((NY - 1,)), dma((6,)),
         ],
         compiler_params=pltpu.CompilerParams(
-            collective_id=0, has_side_effects=True, vmem_limit_bytes=62 << 20
+            collective_id=0, has_side_effects=True, vmem_limit_bytes=52 << 20
         ),
         cost_estimate=pl.CostEstimate(flops=4 * SLOTS * D * H, bytes_accessed=2 * D * H, transcendentals=0),
     )(

time: 112 us -> 107 us (0.955)
  Pallas kernels: 106 us -> 102 us
    pallas_call x1, Pallas kernels: 106 us -> 102 us  [on_device(): pl.pallas_call(kernel, out_shape=(jax.ShapeDtypeStruct((OWN, H), BF), jax...]
    unnamed x3 -> x9, local copies, waits for them, and re-layouts: 4.86 us -> 4.47 us
where the time goes in v3:
time: 107 us
  Pallas kernels  102 us (95%)
  local copies, waits for them, and re-layouts  4.47 us (4%)
    pallas_call x1, Pallas kernels, on_device(): pl.pallas_call(kernel, out_shape=(jax.ShapeDtypeStruct((OWN, H), BF), jax...  102 us
    unnamed x9, local copies, waits for them, and re-layouts  4.47 us

profile of v3, /device:TPU:1, one launch (start us, length us, event | category | flops | bytes accessed | tf_op | source)
XLA Modules:
  0.0 106.9 jit_solution(12947957551795181708)
XLA Ops:
  0.6 0.0 copy-start
  0.6 1.0 copy-done
  1.6 0.0 copy-start.1
  1.6 0.7 copy-done.1
  2.3 0.0 copy-start.2
  2.3 0.7 copy-done.2
  3.0 101.8 %shard_map.76 = (bf16[224,1024]{1,0:T(8,128)(2,1)S(1)}, bf16[192,1024]{1,0:T(8,128)(2,1)S(1)}, f32[8,128]{1,0:T(8,128)S(1)}) custom-call(bf16[128,3584]{1,0:T(8,128)(2,1)} %og_hbm.1, s32[8,128]{1,0:T(8,128)S(1)} %bitcast.11, f32[8,128]{1,0:T(8,128)S(1)} %bitcast.12, bf16[192,1024]{1,0:T(8,128)(2,1)S(1)} %bitcast.10, bf16[3584,1024]{1,0:T(8,128)(2,1)} %bitcast.13), custom_call_target="tpu_custom_call" | custom-call | flops 2818572288 | bytes 7340032 | tf_op jit(solution)/shard_map/pallas_call | solution.py:450
  104.8 0.8 copy.11
  105.6 0.7 copy.12
  106.3 0.6 copy.13
Async XLA Ops:
  0.6 1.0 copy-start
  1.6 0.7 copy-start.1
  2.3 0.7 copy-start.2

commit v4 on v3

--- a/solution.py
+++ b/solution.py
@@ -383,6 +383,33 @@
     gd_s[...] = down.astype(BF)
     gd_out = pltpu.make_async_copy(gd_s, gd_hbm, out_sem.at[1])
     gd_out.start()
+
+    h_copies().wait_send()
+
+    def drain_z(c, carry):
+        z_copies(c).wait_send()
+        return carry
+
+    def drain_p(c, carry):
+        plane_copies(c).wait_send()
+        return carry
+
+    def drain_x(b, carry):
+        x_copies(b).wait_send()
+        return carry
+
+    def drain_y(b, carry):
+        y_copy(b).wait_send()
+        return carry
+
+    lax.fori_loop(0, SPLIT, drain_z, 0)
+    z_copies(SPLIT, 0, 128, NCH).wait_send()
+    z_copies(SPLIT, 128, 128 * (FOLD - 1)).wait_send()
+    lax.fori_loop(SPLIT + 1, NCH, drain_z, 0)
+    lax.fori_loop(0, NCH, drain_p, 0)
+    lax.fori_loop(0, NY, drain_x, 0)
+    lax.fori_loop(0, NY - 1, drain_y, 0)
+    r1_all.wait_send()
 
     some = pl.ds(0, (NJ - 1) * NZ)
     r2_all = remote(r2r.at[some], r2r.at[some], r_sem.at[3], r_sem.at[4], to_j(j))
@@ -409,33 +436,6 @@
     lg_s[...] = scores * (1.0 - scores) * (2.5 / score_sum) * (combine_grad - mean)
     lg_out = pltpu.make_async_copy(lg_s, lg_hbm, out_sem.at[2])
     lg_out.start()
-
-    h_copies().wait_send()
-
-    def drain_z(c, carry):
-        z_copies(c).wait_send()
-        return carry
-
-    def drain_p(c, carry):
-        plane_copies(c).wait_send()
-        return carry
-
-    def drain_x(b, carry):
-        x_copies(b).wait_send()
-        return carry
-
-    def drain_y(b, carry):
-        y_copy(b).wait_send()
-        return carry
-
-    lax.fori_loop(0, SPLIT, drain_z, 0)
-    z_copies(SPLIT, 0, 128, NCH).wait_send()
-    z_copies(SPLIT, 128, 128 * (FOLD - 1)).wait_send()
-    lax.fori_loop(SPLIT + 1, NCH, drain_z, 0)
-    lax.fori_loop(0, NCH, drain_p, 0)
-    lax.fori_loop(0, NY, drain_x, 0)
-    lax.fori_loop(0, NY - 1, drain_y, 0)
-    r1_all.wait_send()
     r2_all.wait_send()
     gh_out.wait()
     gd_out.wait()

time: 107 us -> 107 us (level)
  no operation moved by 1% of the time
where the time goes in v4:
time: 107 us
  Pallas kernels  102 us (95%)
  local copies, waits for them, and re-layouts  4.47 us (4%)
    pallas_call x1, Pallas kernels, on_device(): pl.pallas_call(kernel, out_shape=(jax.ShapeDtypeStruct((OWN, H), BF), jax...  102 us
    unnamed x9, local copies, waits for them, and re-layouts  4.47 us

profile of v4, /device:TPU:1, one launch (start us, length us, event | category | flops | bytes accessed | tf_op | source)
XLA Modules:
  0.0 106.9 jit_solution(12635304506918556984)
XLA Ops:
  0.6 0.0 copy-start
  0.6 1.0 copy-done
  1.6 0.0 copy-start.1
  1.6 0.7 copy-done.1
  2.3 0.0 copy-start.2
  2.3 0.7 copy-done.2
  3.0 101.7 %shard_map.76 = (bf16[224,1024]{1,0:T(8,128)(2,1)S(1)}, bf16[192,1024]{1,0:T(8,128)(2,1)S(1)}, f32[8,128]{1,0:T(8,128)S(1)}) custom-call(bf16[128,3584]{1,0:T(8,128)(2,1)} %og_hbm.1, s32[8,128]{1,0:T(8,128)S(1)} %bitcast.11, f32[8,128]{1,0:T(8,128)S(1)} %bitcast.12, bf16[192,1024]{1,0:T(8,128)(2,1)S(1)} %bitcast.10, bf16[3584,1024]{1,0:T(8,128)(2,1)} %bitcast.13), custom_call_target="tpu_custom_call" | custom-call | flops 2818572288 | bytes 7340032 | tf_op jit(solution)/shard_map/pallas_call | solution.py:450
  104.7 0.8 copy.11
  105.5 0.7 copy.12
  106.3 0.6 copy.13
Async XLA Ops:
  0.6 1.0 copy-start
  1.6 0.7 copy-start.1
  2.3 0.7 copy-start.2
